TPU v7x, 128 devices: a whole 4x4x4 slice. The times are simulated.
128 devices in a mesh: dp: 16 (over x, z), tensor: 8 (over y, core).
Axes of the slice: x: 4, y: 4, z: 4, core: 2. Of those that a mesh axis runs over, the one named last changes fastest.
Arguments:
- gradients: bfloat16 [16, 2304, 24576], P('dp', None, 'tensor'), as said below
- dither: int32 [16, 2304], P('dp'), may hold values from 0 to 1023
- sign_bits: int32 [24576], P('tensor'), may hold values from 0 to 1
Outputs:
- mean_gradient: bfloat16 [2304, 24576], P('dp', 'tensor')
Inputs may be any that keep to these rules, and one draw needn't show every extreme that they name: `gradients`: one gradient matrix a replica; entries bounded.
All inputs are finite; a program needn't handle non-finite values.
Results may differ from a plain program's by a relative error of at most 0.006.
Values may be sent and summed in bfloat16 or wider, within the bound.
A program may use at most 192 MiB of HBM per device.

v0:
```python
import jax
import jax.numpy as jnp
from jax import lax
from jax.sharding import PartitionSpec as P

BLOCK = 1024
LEVELS = 127


def hadamard_table(length):
    table = jnp.ones((1, 1), jnp.float32)
    while table.shape[0] < length:
        upper = jnp.concatenate([table, table], axis=1)
        lower = jnp.concatenate([table, -table], axis=1)
        table = jnp.concatenate([upper, lower], axis=0)
    return table


def local(gradients, dither, sign_bits):
    replicas = lax.axis_size("dp")
    shard_grad = gradients[0]
    row_count, col_count = shard_grad.shape
    blocks = col_count // BLOCK
    hadamard = hadamard_table(BLOCK)
    flips = (1 - 2 * sign_bits).astype(jnp.bfloat16)
    flipped = (shard_grad * flips).reshape(row_count * blocks, BLOCK)
    rotated = jnp.dot(flipped, hadamard.astype(jnp.bfloat16), preferred_element_type=jnp.float32)
    rotated = rotated.reshape(row_count, blocks, BLOCK)
    own_peak = jnp.max(jnp.abs(rotated))
    global_peak = lax.pmax(own_peak, ("dp", "tensor"))
    position = jnp.arange(BLOCK, dtype=jnp.int32)
    offsets = dither[0]
    uniform = (
        ((offsets[:, None, None] + 7919 * position[None, None, :]) % BLOCK).astype(jnp.float32)
        + 0.5
    ) / BLOCK
    quantized = jnp.floor(rotated * (LEVELS / global_peak) + uniform).reshape(row_count, col_count)
    flips_wide = 1.0 - 2.0 * sign_bits.astype(jnp.float32)
    factor = global_peak / (LEVELS * replicas * BLOCK)
    summed = lax.psum_scatter(
        quantized.astype(jnp.bfloat16), "dp", scatter_dimension=0, tiled=True
    ).astype(jnp.float32)
    item_count = summed.shape[0]
    mixed_rows = jnp.einsum(
        "kbi,ij->kbj",
        summed.reshape(item_count, blocks, BLOCK),
        hadamard,
        precision=lax.Precision.HIGHEST,
    )
    return ((mixed_rows * factor).reshape(item_count, col_count) * flips_wide).astype(jnp.bfloat16)


def solution(mesh):
    return jax.shard_map(
        local,
        mesh=mesh,
        in_specs=(P("dp", None, "tensor"), P("dp", None), P("tensor")),
        out_specs=P("dp", "tensor"),
        check_vma=False,
    )
```

profile of v0, /device:TPU:0, one launch (start us, length us, event | category | flops | bytes accessed | tf_op | source)
XLA Modules:
  0.0 265.9 jit_solution(17698464222500382251)
XLA Ops:
  6.5 0.0 reduce-scatter.2.cloned.1.call-start
  6.5 0.0 copy-start
  6.5 0.0 copy-start.2
  6.5 18.0 %copy.5 = bf16[1,2304,3072]{1,2,0:T(8,128)(2,1)} copy(bf16[1,2304,3072]{2,1,0:T(8,128)(2,1)} %param.3) | data formatting | bytes 28311552 | tf_op args[0]
  24.6 0.0 copy-done
  24.6 0.0 copy-done.2
  24.6 0.0 copy-start.1
  24.6 22.6 %abs_reduce_fusion = (f32[]{:T(128)}, f32[2304,3,1024]{0,2,1:T(8,128)}) fusion(bf16[1024,1024,1]{0,1,2:T(8,128)(2,1)S(1)} %copy-done.2, bf16[2304,3,1024]{0,2,1:T(8,128)(2,1)} %bitcast.14, bf16[3,1024]{1,0:T(4,128)(2,1)S(1)} %mul.57), kind=kOutput, calls=%fused_computation.1 | convolution fusion | flops 14537981952 | bytes 44570628 | tf_op jit(solution)/shard_map/dot_general | solution.py:27
  47.2 68.4 %pmax.7 = f32[]{:T(128)} all-reduce(f32[]{:T(128)} %get-tuple-element.5), channel_id=1, replica_groups=mesh['dp'=16,'tensor'=8] {'dp','tensor'}, use_global_device_ids=true, to_apply=%region_1.0 | all-reduce | flops 1 | bytes 8 | tf_op jit(solution)/shard_map/pmax | solution.py:30
  116.3 0.0 copy-done.1
  116.3 4.7 %fusion.4 = f32[2304,1024]{0,1:T(8,128)S(1)} fusion(s32[1024]{0:T(1024)S(1)} %iota_multiply_fusion, s32[2304]{0:T(1024)S(1)} %reduce), kind=kLoop, calls=%fused_computation.11 | loop fusion | flops 35389440 | bytes 9450496 | tf_op jit(solution)/shard_map/div | solution.py:33
  121.0 16.6 %floor_convert_fusion = bf16[2304,3,1024]{0,2,1:T(8,128)(2,1)} fusion(f32[2304,3,1024]{0,2,1:T(8,128)} %get-tuple-element.6, f32[2304,1024]{0,1:T(8,128)S(1)} %fusion.4, f32[]{:T(128)S(6)} %div.12), kind=kLoop, calls=%fused_computation | loop fusion | flops 28311552 | bytes 51904516 | tf_op jit(solution)/shard_map/convert_element_type | solution.py:41
  137.6 18.6 %copy.7 = bf16[2304,3072]{1,0:T(8,128)(2,1)} copy(bf16[2304,3072]{0,1:T(8,128)(2,1)} %bitcast.13) | data formatting | bytes 28311552 | tf_op jit(solution)/shard_map/convert_element_type | solution.py:41
  156.3 0.0 reduce-scatter.2.cloned.1.call-update
  157.0 95.5 %reduce-scatter.2.cloned.1.call-done = bf16[144,3072]{1,0:T(8,128)(2,1)} async-done(((bf16[2304,3072]{1,0:T(8,128)(2,1)}), bf16[144,3072]{1,0:T(8,128)(2,1)}) %reduce-scatter.2.cloned.1.call-update) | async-done | bytes 884752 | tf_op jit(solution)/shard_map/reduce_scatter | solution.py:40
  252.5 5.4 %multiply_bitcast_fusion = f32[3,18,8,1024]{3,2,1,0:T(8,128)S(1)} fusion(f32[1024,1024,1]{1,0,2:T(8,128)} %constant.52, bf16[18,3,8,1024]{3,2,1,0:T(8,128)(2,1)} %bitcast.16, f32[]{:T(128)S(6)} %div.15), kind=kOutput, calls=%fused_computation.15 | convolution fusion | flops 5436260352 | bytes 6848516 | tf_op jit(solution)/shard_map/kbi,ij->kbj/dot_general | solution.py:44
  257.9 0.1 copy.12
  258.0 1.1 multiply_convert_fusion
  (5 shorter events, 0.1 us)
Async XLA Ops:
  6.5 245.9 %reduce-scatter.2.cloned.1.call-start = ((), (), s32[]{:S(2)}) async-start(), calls=%async_computation.1 | async-start | bytes 15040512 | tf_op jit(solution)/shard_map/reduce_scatter | solution.py:40
  6.5 18.0 %copy-start = (s32[3072]{0:T(1024)S(1)}, s32[3072]{0:T(1024)}, u32[]{:S(2)}) copy-start(s32[3072]{0:T(1024)} %param.5) | copy-start | bytes 36868
  6.5 18.1 %copy-start.2 = (bf16[1024,1024,1]{0,1,2:T(8,128)(2,1)S(1)}, bf16[1024,1024,1]{0,1,2:T(8,128)(2,1)}, u32[]{:S(2)}) copy-start(bf16[1024,1024,1]{0,1,2:T(8,128)(2,1)} %constant.51) | copy-start | bytes 6291460
  24.6 91.7 %copy-start.1 = (s32[1,2304]{1,0:T(1,128)S(1)}, s32[1,2304]{1,0:T(1,128)}, u32[]{:S(2)}) copy-start(s32[1,2304]{1,0:T(1,128)} %param.4) | copy-start | bytes 27652
Sparse Core Ops, SparseCore 0:
  156.4 96.0 reduce-scatter.1
where the time goes:
time: 268 us; the launch traced here: 266 us
  waiting for transfers between devices  95.5 us (36%)
  blocking collectives  68.4 us (26%)
  local copies, waits for them, and re-layouts  36.8 us (14%)
  matrix products  28 us (10%)
  other arithmetic  22.4 us (8%)
  between operations  14.8 us (6%)
    reduce_scatter x1, waiting for transfers between devices, local(): lax.psum_scatter(quantized.astype(jnp.bfloat16), 'dp', scatter_dimension=...  95.5 us
    pmax x1, blocking collectives, local(): global_peak = lax.pmax(own_peak, ('dp', 'tensor'))  68.4 us
    dot_general x1, matrix products, local(): jnp.dot(flipped, hadamard.astype(jnp.bfloat16), preferred_element_type=jn...  22.6 us
    convert_element_type x1, local copies, waits for them, and re-layouts, local(): quantized.astype(jnp.bfloat16)  18.6 us
    unnamed x7, local copies, waits for them, and re-layouts  18 us
    convert_element_type x1, other arithmetic, local(): quantized.astype(jnp.bfloat16)  16.6 us
    dot_general x1, matrix products, local(): jnp.einsum('kbi,ij->kbj', summed.reshape(item_count, blocks, BLOCK), hada...  5.44 us
  transfers between devices with their start and end apart: 1, of which 1 were waited for; matrix products, arithmetic and copies ran while one was open for 0% of the time, Pallas kernels for 0%

commit v1 on v0

v1 whole, which is shorter than its diff:
```python
import functools

import jax
import jax.numpy as jnp
from jax import lax
from jax.experimental import pallas as pl
from jax.experimental.pallas import tpu as pltpu
from jax.sharding import PartitionSpec as P

BLOCK = 1024
LEVELS = 127
SIDE = 4
SUB = 256
LANES = 128
MESH = pl.DeviceIdType.MESH

GROUPS = ((0, 0, 0, 144, 0), (1, 2, 0, 144, 224), (0, 1, 0, 80, 144), (1, 1, 80, 64, 368))
PIECES = (
    (0, 0, 0, 48, 0), (1, 2, 0, 48, 224),
    (0, 0, 48, 48, 48), (1, 2, 48, 48, 272),
    (0, 0, 96, 48, 96), (1, 2, 96, 48, 320),
    (0, 1, 0, 48, 144), (1, 1, 80, 32, 368),
    (0, 1, 48, 32, 192), (1, 1, 112, 32, 400),
)
ROWS = 432


def butterfly(parts):
    a, b = parts[0] + parts[1], parts[0] - parts[1]
    c, d = parts[2] + parts[3], parts[2] - parts[3]
    return [a + c, b + d, a - c, b - d]


def kernel(grad, dither_ref, sign_ref, out_ref, held, weights, table, own_dither, near_raw, near_dither, ramp, peak_send,
           peak_recv, peak_ref, raw, first_send, first_recv, partial, second_raw, second_send, second_recv,
           load_sem, near_ss, near_rs, peak_ss, peak_rs, raw_ss, raw_rs, first_ss, first_rs, mid_ss, mid_rs, last_ss, last_rs):
    dp, tensor = lax.axis_index("dp"), lax.axis_index("tensor")
    x, z = dp // SIDE, dp % SIDE

    def along_x(step):
        return ((x + step) % SIDE * SIDE + z, tensor)

    def along_z(step):
        return (x * SIDE + (z + step) % SIDE, tensor)

    def neighbour(axis, step):
        return along_x(step) if axis == 0 else along_z(step)

    stages = (
        [(dp, (tensor + i) % 8) for i in range(1, 8)],
        [along_x(i) for i in range(1, SIDE)],
        [along_z(i) for i in range(1, SIDE)],
    )
    barrier = pltpu.get_barrier_semaphore()
    for stage in stages:
        for peer in stage:
            pl.semaphore_signal(barrier, inc=1, device_id=peer, device_id_type=MESH)

    def load(c):
        return pltpu.make_async_copy(grad.at[c // SIDE, c % SIDE], held.at[c // SIDE, c % SIDE], load_sem.at[c])

    def start_load(c, carry):
        load(c).start()
        return carry

    lax.fori_loop(0, SIDE * SIDE, start_load, 0)

    bits = lax.broadcasted_iota(jnp.int32, (SUB, SUB), 0) & lax.broadcasted_iota(jnp.int32, (SUB, SUB), 1)
    bits = bits ^ (bits >> 4)
    bits = bits ^ (bits >> 2)
    bits = bits ^ (bits >> 1)
    base = (1 - 2 * (bits & 1)).astype(jnp.float32).astype(jnp.bfloat16)
    table[...] = base
    diagonal = lax.broadcasted_iota(jnp.int32, (SUB, SUB), 0) == lax.broadcasted_iota(jnp.int32, (SUB, SUB), 1)
    for i in range(12):
        flips = (1 - 2 * sign_ref[:, i * SUB:(i + 1) * SUB]).astype(jnp.float32)
        scaled = jnp.where(diagonal, flips, 0.0).astype(jnp.bfloat16)
        weights[i // SIDE, i % SIDE] = jnp.dot(scaled, base, preferred_element_type=jnp.float32).astype(jnp.bfloat16)
    column = lax.broadcasted_iota(jnp.int32, (1, BLOCK), 1)
    ramp[...] = (((7919 * column) & (BLOCK - 1)).astype(jnp.float32) + 0.5) * (1.0 / BLOCK)

    pl.semaphore_wait(barrier, 13)

    raw_copies = []
    for g, (h, b, r0, n, q) in enumerate(GROUPS):
        far = (x + 2) % SIDE if h == 0 else (z + 2) % SIDE
        for e in range(2):
            pair = pl.ds(2 * e, 2)
            rows, cols = pl.ds(r0, n), pl.ds(b * BLOCK, BLOCK)
            source = grad.at[far, pair, rows, cols] if h == 0 else grad.at[pair, far, rows, cols]
            copy = pltpu.make_async_remote_copy(
                source, raw.at[e, :, pl.ds(q, n), :], raw_ss.at[2 * g + e], raw_rs.at[2 * g + e],
                device_id=neighbour(h, 2 * e - 1), device_id_type=MESH)
            copy.start()
            raw_copies.append(copy)
    near_copies = []
    for i in range(4):
        copy = pltpu.make_async_remote_copy(
            dither_ref, near_raw.at[i], near_ss.at[i], near_rs.at[i],
            device_id=neighbour(i // 2, 2 * (i % 2) - 1), device_id_type=MESH)
        copy.start()
        near_copies.append(copy)

    def parts_of(ref, lead, rows, b, first):
        return [
            jnp.dot(ref[lead + (rows, pl.ds(first + k * SUB, SUB))], weights[b, k], preferred_element_type=jnp.float32)
            for k in range(SIDE)
        ]

    def peak_of(c, top):
        load(c).wait()
        for b in range(3):
            m = parts_of(held, (c // SIDE, c % SIDE), slice(None), b, b * BLOCK)
            even = jnp.abs(m[0] + m[1]) + jnp.abs(m[2] + m[3])
            odd = jnp.abs(m[0] - m[1]) + jnp.abs(m[2] - m[3])
            both = jnp.maximum(even, odd)
            both = jnp.maximum(both[:, :LANES], both[:, LANES:])
            top = jnp.maximum(top, jnp.max(both.reshape(18, 8, LANES), axis=0))
        return top

    top = lax.fori_loop(0, SIDE * SIDE, peak_of, jnp.zeros((8, LANES), jnp.float32))

    def spread(source, target):
        turned = jnp.transpose(source, (1, 0))[:144]
        for c in range(SIDE * SIDE):
            target[c // SIDE, c % SIDE] = jnp.broadcast_to(turned[:, c:c + 1], (144, LANES))

    done = 0
    peak_copies = []
    for s, stage in enumerate(stages):
        peak_send[s] = top
        copies = []
        for i, peer in enumerate(stage):
            copy = pltpu.make_async_remote_copy(
                peak_send.at[s], peak_recv.at[done + i], peak_ss.at[done + i], peak_rs.at[done + i],
                device_id=peer, device_id_type=MESH)
            copy.start()
            copies.append(copy)
        if s == 0:
            spread(dither_ref[...], own_dither)
            for i in range(4):
                near_copies[i].wait_recv()
                spread(near_raw[i], near_dither.at[i])
        for i, copy in enumerate(copies):
            copy.wait_recv()
        for i in range(len(stage)):
            top = jnp.maximum(top, peak_recv[done + i])
        done += len(stage)
        peak_copies += copies
    top = jnp.max(jnp.max(top, axis=1, keepdims=True), axis=0, keepdims=True)
    peak = jnp.broadcast_to(top, (8, LANES))
    peak_ref[0] = LEVELS / peak
    peak_ref[1] = peak / (LEVELS * 16 * BLOCK)

    def codes(ref, lead, rows, b, first, offsets):
        values = butterfly(parts_of(ref, lead, rows, b, first))
        scale = peak_ref[0, 0:1, :]
        result = []
        for i in range(8):
            shift = offsets + ramp[:, i * LANES:(i + 1) * LANES]
            shift = shift - jnp.floor(shift)
            value = values[i // 2][:, (i % 2) * LANES:(i % 2 + 1) * LANES]
            result.append(jnp.floor(value * scale + shift))
        return result

    def own_codes(h, target, j, b, r0, n):
        lead = (target, j) if h == 0 else (j, target)
        rows = pl.ds(r0, n)
        return codes(held, lead, rows, b, b * BLOCK, own_dither[lead + (rows, slice(None))])

    def lanes(i):
        return slice(i * LANES, (i + 1) * LANES)

    for copy in raw_copies:
        copy.wait_recv()

    first_copies = []
    for p, (h, b, r0, n, q) in enumerate(PIECES):
        here = x if h == 0 else z
        for e in range(2):
            target = (here + 2 * e + 3) % SIDE

            def fill(jj, carry):
                j = 2 * e + jj
                mine = own_codes(h, target, j, b, r0, n)
                lead = (target, j) if h == 0 else (j, target)
                other = codes(raw, (e, jj), pl.ds(q, n), b, 0, near_dither[(2 * h + e,) + lead + (pl.ds(r0, n), slice(None))])
                for i in range(8):
                    first_send[e, j, pl.ds(q, n), lanes(i)] = (mine[i] + other[i]).astype(jnp.bfloat16)
                j = 2 * (1 - e) + jj
                mine = own_codes(h, target, j, b, r0, n)
                for i in range(8):
                    first_send[e, j, pl.ds(q, n), lanes(i)] = mine[i].astype(jnp.bfloat16)
                return carry

            lax.fori_loop(0, 2, fill, 0)
            copy = pltpu.make_async_remote_copy(
                first_send.at[e, :, pl.ds(q, n), :], first_recv.at[e, :, pl.ds(q, n), :],
                first_ss.at[2 * p + e], first_rs.at[2 * p + e],
                device_id=neighbour(h, 2 * e - 1), device_id_type=MESH)
            copy.start()
            first_copies.append(copy)

    mid_copies, last_copies = [], []

    def combine(p):
        h, b, r0, n, q = PIECES[p]
        here, there = (x, z) if h == 0 else (z, x)
        rows = pl.ds(q, n)
        for e in range(2):
            first_copies[2 * p + e].wait_recv()

        def fill(jj, carry):
            j = (there + 2 + jj) % SIDE
            mine = own_codes(h, here, j, b, r0, n)
            for i in range(8):
                total = mine[i]
                for e in range(2):
                    total += first_recv[e, j, rows, lanes(i)].astype(jnp.float32)
                partial[j, rows, lanes(i)] = total.astype(jnp.int32).astype(jnp.int16)
            return carry

        lax.fori_loop(0, 1, fill, 0)
        for e in range(2):
            copy = pltpu.make_async_remote_copy(
                partial.at[(there + 2) % SIDE, rows, pl.ds(512 * e, 512)], second_raw.at[e, rows, :],
                mid_ss.at[2 * p + e], mid_rs.at[2 * p + e],
                device_id=neighbour(1 - h, 2 * e - 1), device_id_type=MESH)
            copy.start()
            mid_copies.append(copy)
        lax.fori_loop(1, SIDE, fill, 0)

    def forward(p):
        h, b, r0, n, q = PIECES[p]
        there = z if h == 0 else x
        rows = pl.ds(q, n)
        for e in range(2):
            mid_copies[2 * p + e].wait_recv()
            j = (there + 2 * e + 3) % SIDE
            plain, summed = pl.ds(512 * (1 - e), 512), pl.ds(512 * e, 512)
            second_send[e, rows, plain] = partial[j, rows, plain]
            total = partial[j, rows, summed].astype(jnp.int32) + second_raw[e, rows, :].astype(jnp.int32)
            second_send[e, rows, summed] = total.astype(jnp.int16)
            copy = pltpu.make_async_remote_copy(
                second_send.at[e, rows, :], second_recv.at[e, rows, :],
                last_ss.at[2 * p + e], last_rs.at[2 * p + e],
                device_id=neighbour(1 - h, 2 * e - 1), device_id_type=MESH)
            copy.start()
            last_copies.append(copy)

    def decode(p):
        h, b, r0, n, q = PIECES[p]
        there = z if h == 0 else x
        rows = pl.ds(q, n)
        for e in range(2):
            last_copies[2 * p + e].wait_recv()
        parts = []
        for k in range(SIDE):
            cols = pl.ds(k * SUB, SUB)
            total = partial[there, rows, cols].astype(jnp.int32)
            for e in range(2):
                total += second_recv[e, rows, cols].astype(jnp.int32)
            total = total.astype(jnp.float32)
            high = total.astype(jnp.bfloat16)
            low = (total - high.astype(jnp.float32)).astype(jnp.bfloat16)
            parts.append(jnp.dot(high, table[...], preferred_element_type=jnp.float32)
                         + jnp.dot(low, table[...], preferred_element_type=jnp.float32))
        values = butterfly(parts)
        factor = peak_ref[1, 0:1, :]
        for i in range(8):
            col = b * BLOCK + i * LANES
            flips = (1 - 2 * sign_ref[:, col:col + LANES]).astype(jnp.float32)
            value = values[i // 2][:, (i % 2) * LANES:(i % 2 + 1) * LANES]
            out_ref[r0:r0 + n, col:col + LANES] = (value * factor * flips).astype(jnp.bfloat16)

    count = len(PIECES)
    for step in range(count + 4):
        if step < count:
            combine(step)
        if 2 <= step < count + 2:
            forward(step - 2)
        if step >= 4:
            decode(step - 4)
    for copy in near_copies + peak_copies + raw_copies + first_copies + mid_copies + last_copies:
        copy.wait_send()


def local(gradients, dither, sign_bits):
    row_count, col_count = gradients.shape[1:]
    grad = gradients.reshape(SIDE, SIDE, row_count // 16, col_count)
    offsets = jnp.pad(dither.astype(jnp.float32).reshape(16, row_count // 16) * (1.0 / BLOCK), ((0, 0), (0, 112)))
    vmem, dma = pltpu.VMEM, pltpu.SemaphoreType.DMA
    pieces = 2 * len(PIECES)
    return pl.pallas_call(
        kernel,
        out_shape=jax.ShapeDtypeStruct((row_count // 16, col_count), jnp.bfloat16),
        in_specs=[pl.BlockSpec(memory_space=pl.ANY)] + [pl.BlockSpec(memory_space=pltpu.VMEM)] * 2,
        out_specs=pl.BlockSpec(memory_space=pltpu.VMEM),
        scratch_shapes=[
            vmem((SIDE, SIDE, 144, col_count), jnp.bfloat16),
            vmem((3, SIDE, SUB, SUB), jnp.bfloat16),
            vmem((SUB, SUB), jnp.bfloat16),
            vmem((SIDE, SIDE, 144, LANES), jnp.float32),
            vmem((4, 16, 256), jnp.float32),
            vmem((4, SIDE, SIDE, 144, LANES), jnp.float32),
            vmem((1, BLOCK), jnp.float32),
            vmem((3, 8, LANES), jnp.float32),
            vmem((13, 8, LANES), jnp.float32),
            vmem((2, 8, LANES), jnp.float32),
            vmem((2, 2, ROWS, BLOCK), jnp.bfloat16),
            vmem((2, SIDE, ROWS, BLOCK), jnp.bfloat16),
            vmem((2, SIDE, ROWS, BLOCK), jnp.bfloat16),
            vmem((SIDE, ROWS, BLOCK), jnp.int16),
            vmem((2, ROWS, 512), jnp.int16),
            vmem((2, ROWS, BLOCK), jnp.int16),
            vmem((2, ROWS, BLOCK), jnp.int16),
            dma((16,)), dma((4,)), dma((4,)), dma((13,)), dma((13,)), dma((8,)), dma((8,)),
            dma((pieces,)), dma((pieces,)), dma((pieces,)), dma((pieces,)), dma((pieces,)), dma((pieces,)),
        ],
        compiler_params=pltpu.CompilerParams(collective_id=0, has_side_effects=True, vmem_limit_bytes=60 * 2**20),
    )(grad, offsets, sign_bits.reshape(1, col_count))


def solution(mesh):
    return jax.shard_map(
        local,
        mesh=mesh,
        in_specs=(P("dp", None, "tensor"), P("dp", None), P("tensor")),
        out_specs=P("dp", "tensor"),
        check_vma=False,
    )
```

time: 268 us -> 108 us (0.40)
  Pallas kernels: 0 us -> 104 us
  waiting for transfers between devices: 95.5 us -> 0 us
  blocking collectives: 68.4 us -> 0 us
  local copies, waits for them, and re-layouts: 36.8 us -> 2.83 us
  matrix products: 28 us -> 0 us
  other arithmetic: 22.4 us -> 0.73 us
  between operations: 14.8 us -> 0.02 us
    pallas_call x0 -> x1, Pallas kernels: none -> 104 us  [local(): pl.pallas_call(kernel, out_shape=jax.ShapeDtypeStruct((row_count // 16, c...]
    reduce_scatter x1 -> x0, waiting for transfers between devices: 95.5 us -> none  [local(): lax.psum_scatter(quantized.astype(jnp.bfloat16), 'dp', scatter_dimension=...]
    pmax x1 -> x0, blocking collectives: 68.4 us -> none  [local(): global_peak = lax.pmax(own_peak, ('dp', 'tensor'))]
    dot_general x2 -> x0, matrix products: 28 us -> none  [the longest x1 22.6 us: local(): jnp.dot(flipped, hadamard.astype(jnp.bfloat16), preferred_element_type=jn...]
    convert_element_type x1 -> x0, local copies, waits for them, and re-layouts: 18.6 us -> none  [local(): quantized.astype(jnp.bfloat16)]
    convert_element_type x3 -> x0, other arithmetic: 17.7 us -> none  [the longest x1 16.6 us: local(): quantized.astype(jnp.bfloat16)]
    unnamed x7 -> x1, local copies, waits for them, and re-layouts: 18 us -> 2.14 us
    div x1 -> x0, other arithmetic: 4.67 us -> none  [local(): (((offsets[:, None, None] + 7919 * position[None, None, :]) % BLOCK).asty...]
  transfers between devices with their start and end apart: 1 -> 0, of which waited for: 1 -> 0; matrix products, arithmetic and copies ran while one was open for 0% -> 0% of each run, Pallas kernels for 0% -> 0%
where the time goes in v1:
time: 108 us
  Pallas kernels  104 us (96%)
  local copies, waits for them, and re-layouts  2.83 us (3%)
    pallas_call x1, Pallas kernels, local(): pl.pallas_call(kernel, out_shape=jax.ShapeDtypeStruct((row_count // 16, c...  104 us

profile of v1, /device:TPU:0, one launch (start us, length us, event | category | flops | bytes accessed | tf_op | source)
XLA Modules:
  0.0 107.7 jit_solution(16101126232963585763)
XLA Ops:
  0.0 0.7 multiply_reduce_fusion
  0.7 0.1 mul.11
  0.8 0.6 pad.4.dither_ref
  1.4 104.2 %shard_map.37 = bf16[144,3072]{1,0:T(8,128)(2,1)} custom-call(bf16[4,4,144,3072]{3,2,1,0:T(8,128)(2,1)} %bitcast.2, f32[16,256]{1,0:T(8,128)} %pad.4.dither_ref, s32[1,3072]{1,0:T(1,128)} %bitcast.3), custom_call_target="tpu_custom_call" | custom-call | tf_op jit(solution)/shard_map/pallas_call | solution.py:294
  105.6 2.1 %copy.5 = bf16[144,3072]{1,0:T(8,128)(2,1)} copy(bf16[144,3072]{1,0:T(8,128)(2,1)} %shard_map.37) | data formatting | bytes 1769472

commit v2 on v1

v2 whole, which is shorter than its diff:
```python
import functools

import jax
import jax.numpy as jnp
from jax import lax
from jax.experimental import pallas as pl
from jax.experimental.pallas import tpu as pltpu
from jax.sharding import PartitionSpec as P

BLOCK = 1024
LEVELS = 127
SIDE = 4
SUB = 256
LANES = 128
MESH = pl.DeviceIdType.MESH

PIECES = (
    (0, 0, 0, 48, 0), (1, 2, 0, 48, 224),
    (0, 0, 48, 48, 48), (1, 2, 48, 48, 272),
    (0, 0, 96, 48, 96), (1, 2, 96, 48, 320),
    (0, 1, 0, 48, 144), (1, 1, 80, 32, 368),
    (0, 1, 48, 32, 192), (1, 1, 112, 32, 400),
)
ROWS = 432
RAW_EARLY = (0, 1, 2, 3, 4, 5, 7)
RAW_LATER = ((), (6, 8), (9,))
LEAVES = {0: 0, 1: 48}
LEAF_LATER = ((), (0,), (1,))
LEAF_ROWS = 96


def butterfly(parts):
    a, b = parts[0] + parts[1], parts[0] - parts[1]
    c, d = parts[2] + parts[3], parts[2] - parts[3]
    return [a + c, b + d, a - c, b - d]


def kernel(grad, dither_in, sign_in, out_ref, dither_ref, sign_ref, held, weights, table, own_dither, near_raw, near_dither, rows_of, ramp, peak_send,
           peak_recv, peak_ref, raw, leaf, first_send, first_recv, partial, second_raw, second_send, second_recv,
           small_sem, load_sem, near_ss, near_rs, peak_ss, peak_rs, raw_ss, raw_rs, leaf_ss, leaf_rs, first_ss, first_rs, mid_ss, mid_rs, last_ss, last_rs):
    dp, tensor = lax.axis_index("dp"), lax.axis_index("tensor")
    x, z = dp // SIDE, dp % SIDE

    def lanes(i):
        return slice(i * LANES, (i + 1) * LANES)

    def along_x(step):
        return ((x + step) % SIDE * SIDE + z, tensor)

    def along_z(step):
        return (x * SIDE + (z + step) % SIDE, tensor)

    def neighbour(axis, step):
        return along_x(step) if axis == 0 else along_z(step)

    stages = (
        [(dp, (tensor + i) % 8) for i in range(1, 8)],
        [along_x(i) for i in range(1, SIDE)],
        [along_z(i) for i in range(1, SIDE)],
    )
    small = [pltpu.make_async_copy(dither_in, dither_ref, small_sem.at[0]),
             pltpu.make_async_copy(sign_in, sign_ref, small_sem.at[1])]
    for copy in small:
        copy.start()
    barrier = pltpu.get_barrier_semaphore()
    for stage in stages:
        for peer in stage:
            pl.semaphore_signal(barrier, inc=1, device_id=peer, device_id_type=MESH)

    def load(c):
        return pltpu.make_async_copy(grad.at[c // SIDE, c % SIDE], held.at[c // SIDE, c % SIDE], load_sem.at[c])

    def start_load(c, carry):
        load(c).start()
        return carry

    lax.fori_loop(0, SIDE * SIDE, start_load, 0)

    pl.semaphore_wait(barrier, 13)

    raw_copies = {}

    def send_raw(p):
        h, b, r0, n, q = PIECES[p]
        far = (x + 2) % SIDE if h == 0 else (z + 2) % SIDE
        for e in range(2):
            pair = pl.ds(2 * e, 2)
            rows, cols = pl.ds(r0, n), pl.ds(b * BLOCK, BLOCK)
            source = grad.at[far, pair, rows, cols] if h == 0 else grad.at[pair, far, rows, cols]
            copy = pltpu.make_async_remote_copy(
                source, raw.at[e, :, pl.ds(q, n), :], raw_ss.at[2 * p + e], raw_rs.at[2 * p + e],
                device_id=neighbour(h, 2 * e - 1), device_id_type=MESH)
            copy.start()
            raw_copies[2 * p + e] = copy

    leaf_copies = {}

    def send_leaf(p):
        h, b, r0, n, q = PIECES[p]
        here = x if h == 0 else z
        for e in range(2):
            target = (here + 2 * e + 3) % SIDE
            pair = pl.ds(2 * (1 - e), 2)
            rows, cols = pl.ds(r0, n), pl.ds(b * BLOCK, BLOCK)
            source = grad.at[target, pair, rows, cols] if h == 0 else grad.at[pair, target, rows, cols]
            copy = pltpu.make_async_remote_copy(
                source, leaf.at[e, :, pl.ds(LEAVES[p], n), :], leaf_ss.at[2 * p + e], leaf_rs.at[2 * p + e],
                device_id=neighbour(h, 2 * e - 1), device_id_type=MESH)
            copy.start()
            leaf_copies[2 * p + e] = copy

    small[0].wait()
    near_copies = []
    for i in range(4):
        copy = pltpu.make_async_remote_copy(
            dither_ref, near_raw.at[i], near_ss.at[i], near_rs.at[i],
            device_id=neighbour(i // 2, 2 * (i % 2) - 1), device_id_type=MESH)
        copy.start()
        near_copies.append(copy)

    for p in RAW_EARLY:
        send_raw(p)

    bits = lax.broadcasted_iota(jnp.int32, (SUB, SUB), 0) & lax.broadcasted_iota(jnp.int32, (SUB, SUB), 1)
    bits = bits ^ (bits >> 4)
    bits = bits ^ (bits >> 2)
    bits = bits ^ (bits >> 1)
    base = (1 - 2 * (bits & 1)).astype(jnp.float32).astype(jnp.bfloat16)
    table[...] = base
    small[1].wait()
    diagonal = lax.broadcasted_iota(jnp.int32, (SUB, SUB), 0) == lax.broadcasted_iota(jnp.int32, (SUB, SUB), 1)
    for i in range(12):
        flips = (1 - 2 * sign_ref[:, i * SUB:(i + 1) * SUB]).astype(jnp.float32)
        scaled = jnp.where(diagonal, flips, 0.0).astype(jnp.bfloat16)
        weights[i // SIDE, i % SIDE] = jnp.dot(scaled, base, preferred_element_type=jnp.float32).astype(jnp.bfloat16)
    column = lax.broadcasted_iota(jnp.int32, (1, BLOCK), 1)
    ramp[...] = (((7919 * column) & (BLOCK - 1)).astype(jnp.float32) + 0.5) * (1.0 / BLOCK)

    def parts_of(ref, lead, b, first):
        parts = []
        for k in range(SIDE):
            values = ref[lead + (pl.ds(first + k * SUB, SUB),)]
            values = values.reshape(-1, SUB)
            parts.append(jnp.dot(values, weights[b, k], preferred_element_type=jnp.float32))
        return parts

    def peak_of(c, top):
        load(2 * c).wait()
        load(2 * c + 1).wait()
        for b in range(3):
            m = parts_of(held, (c // 2, pl.ds(c % 2 * 2, 2), slice(None)), b, b * BLOCK)
            even = jnp.abs(m[0] + m[1]) + jnp.abs(m[2] + m[3])
            odd = jnp.abs(m[0] - m[1]) + jnp.abs(m[2] - m[3])
            both = jnp.maximum(even, odd)
            both = jnp.maximum(both[:, :LANES], both[:, LANES:])
            top = jnp.maximum(top, jnp.max(both.reshape(36, 8, LANES), axis=0))
        return top

    top = lax.fori_loop(0, SIDE * 2, peak_of, jnp.zeros((8, LANES), jnp.float32))

    def spread(source, target):
        for i in range(18):
            rows_of[i:i + 1, :] = source[:, lanes(i)].astype(jnp.float32) * (1.0 / BLOCK)
        turned = jnp.transpose(rows_of[...], (1, 0))
        for i in range(18):
            spread_rows = jnp.broadcast_to(turned[:, i:i + 1], (LANES, LANES))
            start = i * LANES
            while start < (i + 1) * LANES:
                c, r = start // 144, start % 144
                n = min(144 - r, (i + 1) * LANES - start)
                target[c // SIDE, c % SIDE, r:r + n, :] = spread_rows[start - i * LANES:start - i * LANES + n]
                start += n

    done = 0
    peak_copies = []
    for s, stage in enumerate(stages):
        peak_send[s] = top
        copies = []
        for i, peer in enumerate(stage):
            copy = pltpu.make_async_remote_copy(
                peak_send.at[s], peak_recv.at[done + i], peak_ss.at[done + i], peak_rs.at[done + i],
                device_id=peer, device_id_type=MESH)
            copy.start()
            copies.append(copy)
        for p in RAW_LATER[s]:
            send_raw(p)
        for p in LEAF_LATER[s]:
            send_leaf(p)
        if s == 0:
            spread(dither_ref, own_dither)
            for i in range(4):
                near_copies[i].wait_recv()
                spread(near_raw.at[i], near_dither.at[i])
        for i, copy in enumerate(copies):
            copy.wait_recv()
        for i in range(len(stage)):
            top = jnp.maximum(top, peak_recv[done + i])
        done += len(stage)
        peak_copies += copies
    top = jnp.max(jnp.max(top, axis=1, keepdims=True), axis=0, keepdims=True)
    peak = jnp.broadcast_to(top, (8, LANES))
    peak_ref[0] = LEVELS / peak
    peak_ref[1] = peak / (LEVELS * 16 * BLOCK)

    def codes(ref, lead, b, first, offsets):
        values = butterfly(parts_of(ref, lead, b, first))
        offsets = offsets.reshape(-1, LANES)
        scale = peak_ref[0, 0:1, :]
        result = []
        for i in range(8):
            shift = offsets + ramp[:, lanes(i)]
            shift = shift - jnp.floor(shift)
            value = values[i // 2][:, (i % 2) * LANES:(i % 2 + 1) * LANES]
            result.append(jnp.floor(value * scale + shift))
        return result

    def pair_of(h, target, j, r0, n):
        pair = pl.ds(j, 2)
        return ((target, pair) if h == 0 else (pair, target)) + (pl.ds(r0, n),)

    def own_codes(h, target, j, b, r0, n):
        lead = pair_of(h, target, j, r0, n)
        return codes(held, lead, b, b * BLOCK, own_dither[lead + (slice(None),)])

    def near_codes(ref, lead, h, e, target, j, b, r0, n):
        return codes(ref, lead, b, 0, near_dither[(2 * h + e,) + pair_of(h, target, j, r0, n) + (slice(None),)])

    first_copies = {}

    def first(p):
        h, b, r0, n, q = PIECES[p]
        here = x if h == 0 else z
        rows = pl.ds(q, n)
        for e in range(2):
            target = (here + 2 * e + 3) % SIDE
            raw_copies[2 * p + e].wait_recv()
            mine = own_codes(h, target, 2 * e, b, r0, n)
            other = near_codes(raw, (e, slice(None), rows), h, e, target, 2 * e, b, r0, n)
            for i in range(8):
                total = (mine[i] + other[i]).astype(jnp.bfloat16)
                first_send[e, pl.ds(2 * e, 2), rows, lanes(i)] = total.reshape(2, n, LANES)
            if p not in LEAVES:
                mine = own_codes(h, target, 2 * (1 - e), b, r0, n)
                for i in range(8):
                    first_send[e, pl.ds(2 * (1 - e), 2), rows, lanes(i)] = mine[i].astype(jnp.bfloat16).reshape(2, n, LANES)
            sent = pl.ds(2 * e, 2) if p in LEAVES else slice(None)
            copy = pltpu.make_async_remote_copy(
                first_send.at[e, sent, rows, :], first_recv.at[e, sent, rows, :],
                first_ss.at[2 * p + e], first_rs.at[2 * p + e],
                device_id=neighbour(h, 2 * e - 1), device_id_type=MESH)
            copy.start()
            first_copies[2 * p + e] = copy

    mid_copies, last_copies = {}, {}

    def combine(p):
        h, b, r0, n, q = PIECES[p]
        here, there = (x, z) if h == 0 else (z, x)
        rows = pl.ds(q, n)
        for e in range(2):
            first_copies[2 * p + e].wait_recv()

        def fill(half):
            pair = pl.ds(2 * half, 2)
            mine = own_codes(h, here, 2 * half, b, r0, n)
            if p in LEAVES:
                mine_too = near_codes(leaf, (1 - half, slice(None), pl.ds(LEAVES[p], n)), h, 1 - half, here, 2 * half, b, r0, n)
            for i in range(8):
                total = mine[i]
                if p in LEAVES:
                    total += mine_too[i] + first_recv[half, pair, rows, lanes(i)].astype(jnp.float32).reshape(2 * n, LANES)
                else:
                    for e in range(2):
                        total += first_recv[e, pair, rows, lanes(i)].astype(jnp.float32).reshape(2 * n, LANES)
                partial[pair, rows, lanes(i)] = total.astype(jnp.int32).astype(jnp.int16).reshape(2, n, LANES)

        def send():
            for e in range(2):
                copy = pltpu.make_async_remote_copy(
                    partial.at[(there + 2) % SIDE, rows, pl.ds(512 * e, 512)], second_raw.at[e, rows, :],
                    mid_ss.at[2 * p + e], mid_rs.at[2 * p + e],
                    device_id=neighbour(1 - h, 2 * e - 1), device_id_type=MESH)
                copy.start()
                mid_copies[2 * p + e] = copy

        if p in LEAVES:
            for e in range(2):
                leaf_copies[2 * p + e].wait_recv()
            fill(0)
            fill(1)
            send()
        else:
            opposite = (there + 2) % SIDE // 2
            fill(opposite)
            send()
            fill(1 - opposite)

    def forward(p):
        h, b, r0, n, q = PIECES[p]
        there = z if h == 0 else x
        rows = pl.ds(q, n)
        for e in range(2):
            mid_copies[2 * p + e].wait_recv()
            j = (there + 2 * e + 3) % SIDE
            plain, summed = pl.ds(512 * (1 - e), 512), pl.ds(512 * e, 512)
            second_send[e, rows, plain] = partial[j, rows, plain]
            total = partial[j, rows, summed].astype(jnp.int32) + second_raw[e, rows, :].astype(jnp.int32)
            second_send[e, rows, summed] = total.astype(jnp.int16)
            copy = pltpu.make_async_remote_copy(
                second_send.at[e, rows, :], second_recv.at[e, rows, :],
                last_ss.at[2 * p + e], last_rs.at[2 * p + e],
                device_id=neighbour(1 - h, 2 * e - 1), device_id_type=MESH)
            copy.start()
            last_copies[2 * p + e] = copy

    def decode(p):
        h, b, r0, n, q = PIECES[p]
        there = z if h == 0 else x
        rows = pl.ds(q, n)
        for e in range(2):
            last_copies[2 * p + e].wait_recv()
        parts = []
        for k in range(SIDE):
            cols = pl.ds(k * SUB, SUB)
            total = partial[there, rows, cols].astype(jnp.int32)
            for e in range(2):
                total += second_recv[e, rows, cols].astype(jnp.int32)
            total = total.astype(jnp.float32)
            high = total.astype(jnp.bfloat16)
            low = (total - high.astype(jnp.float32)).astype(jnp.bfloat16)
            parts.append(jnp.dot(high, table[...], preferred_element_type=jnp.float32)
                         + jnp.dot(low, table[...], preferred_element_type=jnp.float32))
        values = butterfly(parts)
        factor = peak_ref[1, 0:1, :]
        for i in range(8):
            col = b * BLOCK + i * LANES
            flips = (1 - 2 * sign_ref[:, col:col + LANES]).astype(jnp.float32)
            value = values[i // 2][:, (i % 2) * LANES:(i % 2 + 1) * LANES]
            out_ref[r0:r0 + n, col:col + LANES] = (value * factor * flips).astype(jnp.bfloat16)

    count = len(PIECES) // 2
    tasks = ((first, 0), (combine, 2), (forward, 3), (decode, 4))
    for step in range(count + 4):
        for task, lag in tasks:
            for p in (2 * (step - lag), 2 * (step - lag) + 1):
                if 0 <= p < len(PIECES):
                    task(p)
    for copies in (raw_copies, leaf_copies, first_copies, mid_copies, last_copies):
        for copy in copies.values():
            copy.wait_send()
    for copy in near_copies + peak_copies:
        copy.wait_send()


def local(gradients, dither, sign_bits):
    row_count, col_count = gradients.shape[1:]
    grad = gradients.reshape(SIDE, SIDE, row_count // 16, col_count)
    vmem, dma = pltpu.VMEM, pltpu.SemaphoreType.DMA
    pieces = 2 * len(PIECES)
    return pl.pallas_call(
        kernel,
        out_shape=jax.ShapeDtypeStruct((row_count // 16, col_count), jnp.bfloat16),
        in_specs=[pl.BlockSpec(memory_space=pltpu.HBM)] * 3,
        out_specs=pl.BlockSpec(memory_space=pltpu.VMEM),
        scratch_shapes=[
            vmem((1, row_count), jnp.int32),
            vmem((1, col_count), jnp.int32),
            vmem((SIDE, SIDE, 144, col_count), jnp.bfloat16),
            vmem((3, SIDE, SUB, SUB), jnp.bfloat16),
            vmem((SUB, SUB), jnp.bfloat16),
            vmem((SIDE, SIDE, 144, LANES), jnp.float32),
            vmem((4, 1, row_count), jnp.int32),
            vmem((4, SIDE, SIDE, 144, LANES), jnp.float32),
            vmem((24, LANES), jnp.float32),
            vmem((1, BLOCK), jnp.float32),
            vmem((3, 8, LANES), jnp.float32),
            vmem((13, 8, LANES), jnp.float32),
            vmem((2, 8, LANES), jnp.float32),
            vmem((2, 2, ROWS, BLOCK), jnp.bfloat16),
            vmem((2, 2, LEAF_ROWS, BLOCK), jnp.bfloat16),
            vmem((2, SIDE, ROWS, BLOCK), jnp.bfloat16),
            vmem((2, SIDE, ROWS, BLOCK), jnp.bfloat16),
            vmem((SIDE, ROWS, BLOCK), jnp.int16),
            vmem((2, ROWS, 512), jnp.int16),
            vmem((2, ROWS, BLOCK), jnp.int16),
            vmem((2, ROWS, BLOCK), jnp.int16),
            dma((2,)), dma((16,)), dma((4,)), dma((4,)), dma((13,)), dma((13,)), dma((pieces,)), dma((pieces,)),
            dma((4,)), dma((4,)), dma((pieces,)), dma((pieces,)), dma((pieces,)), dma((pieces,)), dma((pieces,)), dma((pieces,)),
        ],
        compiler_params=pltpu.CompilerParams(collective_id=0, has_side_effects=True, vmem_limit_bytes=50 * 2**20),
    )(grad, dither, sign_bits.reshape(1, col_count))


def solution(mesh):
    return jax.shard_map(
        local,
        mesh=mesh,
        in_specs=(P("dp", None, "tensor"), P("dp", None), P("tensor")),
        out_specs=P("dp", "tensor"),
        check_vma=False,
    )
```

time: 108 us -> 89.4 us (0.83)
  Pallas kernels: 104 us -> 86.7 us
    pallas_call x1, Pallas kernels: 104 us -> 86.7 us  [local(): pl.pallas_call(kernel, out_shape=jax.ShapeDtypeStruct((row_count // 16, c...]
    unnamed x1 -> x5, local copies, waits for them, and re-layouts: 2.14 us -> 2.32 us
where the time goes in v2:
time: 89.4 us; the launch traced here: 89.1 us
  Pallas kernels  86.7 us (97%)
  local copies, waits for them, and re-layouts  2.32 us (3%)
    pallas_call x1, Pallas kernels, local(): pl.pallas_call(kernel, out_shape=jax.ShapeDtypeStruct((row_count // 16, c...  86.7 us
    unnamed x5, local copies, waits for them, and re-layouts  2.32 us

profile of v2, /device:TPU:0, one launch (start us, length us, event | category | flops | bytes accessed | tf_op | source)
XLA Modules:
  0.0 89.1 jit_solution(4337503440991752213)
XLA Ops:
  0.0 0.0 copy-start
  0.0 0.7 copy-done
  0.7 0.0 copy-start.1
  0.7 0.7 copy-done.1
  1.4 86.7 %shard_map.37 = bf16[144,3072]{1,0:T(8,128)(2,1)S(1)} custom-call(bf16[4,4,144,3072]{3,2,1,0:T(8,128)(2,1)} %bitcast.3, s32[1,2304]{1,0:T(1,128)S(1)} %copy-done.1, s32[1,3072]{1,0:T(1,128)S(1)} %bitcast.2), custom_call_target="tpu_custom_call" | custom-call | tf_op jit(solution)/shard_map/pallas_call | solution.py:360
  88.2 0.9 %copy.5 = bf16[144,3072]{1,0:T(8,128)(2,1)} copy(bf16[144,3072]{1,0:T(8,128)(2,1)S(1)} %shard_map.37) | data formatting | bytes 1769472
Async XLA Ops:
  0.0 0.7 copy-start
  0.7 0.7 copy-start.1

commit v3 on v2

v3 whole, which is shorter than its diff:
```python
import functools

import jax
import jax.numpy as jnp
from jax import lax
from jax.experimental import pallas as pl
from jax.experimental.pallas import tpu as pltpu
from jax.sharding import PartitionSpec as P

BLOCK = 1024
LEVELS = 127
SIDE = 4
SUB = 256
LANES = 128
MESH = pl.DeviceIdType.MESH

PIECES = (
    (0, 0, 0, 48, 0), (1, 2, 0, 48, 224),
    (0, 0, 48, 48, 48), (1, 2, 48, 48, 272),
    (0, 0, 96, 48, 96), (1, 2, 96, 48, 320),
    (0, 1, 0, 48, 144), (1, 1, 80, 32, 368),
    (0, 1, 48, 32, 192), (1, 1, 112, 32, 400),
)
ROWS = 432
ORDER = ((0, 0), (0, 1), (0, 2), (0, 3), (1, 0), (0, 4), (1, 1), (1, 2), (2, 0), (1, 3), (2, 1), (1, 4), (2, 2), (3, 0), (2, 3), (2, 4), (3, 1), (3, 2), (3, 3), (3, 4))
RAW_EARLY = (0, 1, 2, 3)
RAW_LATE = (4, 5, 6, 7, 8, 9)
LEAVES = {0: 0, 1: 48, 2: 96, 3: 144}
LEAF_ROWS = 192


def butterfly(parts):
    a, b = parts[0] + parts[1], parts[0] - parts[1]
    c, d = parts[2] + parts[3], parts[2] - parts[3]
    return [a + c, b + d, a - c, b - d]


def kernel(grad, small_in, out_ref, dither_ref, sign_ref, held, weights, table, own_dither, near_raw, near_dither, rows_of, ramp, peak_send,
           peak_recv, peak_all, peak_ref, raw, leaf, first_send, first_recv, partial, second_raw, second_send, second_recv,
           small_sem, load_sem, near_ss, near_rs, peak_ss, peak_rs, raw_ss, raw_rs, leaf_ss, leaf_rs, first_ss, first_rs, mid_ss, mid_rs, last_ss, last_rs):
    dp, tensor = lax.axis_index("dp"), lax.axis_index("tensor")
    x, z = dp // SIDE, dp % SIDE

    def lanes(i):
        return slice(i * LANES, (i + 1) * LANES)

    core = tensor % 2
    turns = (core, 1 - core)

    def place(step_x, step_z, step_t):
        return ((x + step_x + SIDE) % SIDE * SIDE + (z + step_z + SIDE) % SIDE, (tensor + step_t + 8) % 8)

    def neighbour(axis, step):
        return place(step * (1 - axis), step * axis, 0)

    def spots(h):
        return x + turns[h] * (z - x), z + turns[h] * (x - z)

    def target_of(h, here, there):
        return here * (SIDE - 3 * turns[h]) + there * (1 + 3 * turns[h])

    stages = (
        [place(i, 0, 0) for i in range(1, SIDE)],
        [place(0, 0, 2 * i) for i in range(1, SIDE)],
        [place(0, i, 2) for i in range(1, SIDE)],
    )
    partner = (dp, tensor + 1 - 2 * core)
    next_to = [place(1, 0, 0), place(-1, 0, 0), place(0, 1, 0), place(0, -1, 0)]
    further = [place(2, 0, 0)] + stages[1] + [place(0, -i, -2) for i in range(1, SIDE)] + [partner]
    barrier = pltpu.get_barrier_semaphore()
    for peer in next_to:
        pl.semaphore_signal(barrier, inc=1, device_id=peer, device_id_type=MESH)

    @pl.when(core == 0)
    def _():
        for peer in further:
            pl.semaphore_signal(barrier, inc=1, device_id=peer, device_id_type=MESH)


    split = dither_ref.shape[1]
    small = [pltpu.make_async_copy(small_in.at[:, pl.ds(0, split)], dither_ref, small_sem.at[0]),
             pltpu.make_async_copy(small_in.at[:, pl.ds(split, sign_ref.shape[1])], sign_ref, small_sem.at[1])]
    for copy in small:
        copy.start()
    def load(c):
        return pltpu.make_async_copy(grad.at[c], held.at[c], load_sem.at[c])

    def start_load(c, carry):
        load(c).start()
        return carry

    pl.semaphore_wait(barrier, 11 - 6 * core)

    def row_copies(p, here, j, buffer, first, e, send_sem, recv_sem):
        h, b, r0, n, q = PIECES[p]
        copies = []
        for jj in range(2):
            i = 4 * p + 2 * e + jj
            copies.append(pltpu.make_async_remote_copy(
                grad.at[target_of(h, here, j + jj), pl.ds(r0, n), pl.ds(b * BLOCK, BLOCK)],
                buffer.at[e, jj, pl.ds(first, n), :], send_sem.at[i], recv_sem.at[i],
                device_id=neighbour(turns[h], 2 * e - 1), device_id_type=MESH))
        return copies

    def raw_copies(p, e):
        far = (spots(PIECES[p][0])[0] + 2) % SIDE
        return row_copies(p, far, 2 * e, raw, PIECES[p][4], e, raw_ss, raw_rs)

    def leaf_copies(p, e):
        target = (spots(PIECES[p][0])[0] + 2 * e + 3) % SIDE
        return row_copies(p, target, 2 * (1 - e), leaf, LEAVES[p], e, leaf_ss, leaf_rs)

    def send_raw(p):
        for e in range(2):
            for copy in raw_copies(p, e):
                copy.start()

    def send_late():
        for p in RAW_LATE:
            send_raw(p)
        for p in LEAVES:
            for e in range(2):
                for copy in leaf_copies(p, e):
                    copy.start()

    for p in RAW_EARLY[:2]:
        send_raw(p)
    lax.fori_loop(0, SIDE * SIDE, start_load, 0)
    small[0].wait()
    near_copies = []
    for i in range(4):
        copy = pltpu.make_async_remote_copy(
            dither_ref, near_raw.at[i], near_ss.at[i], near_rs.at[i],
            device_id=neighbour(turns[i // 2], 2 * (i % 2) - 1), device_id_type=MESH)
        copy.start()
        near_copies.append(copy)

    for p in RAW_EARLY[2:]:
        send_raw(p)
    pl.when(core == 1)(send_late)

    bits = lax.broadcasted_iota(jnp.int32, (SUB, SUB), 0) & lax.broadcasted_iota(jnp.int32, (SUB, SUB), 1)
    bits = bits ^ (bits >> 4)
    bits = bits ^ (bits >> 2)
    bits = bits ^ (bits >> 1)
    base = (1 - 2 * (bits & 1)).astype(jnp.float32).astype(jnp.bfloat16)
    table[...] = base
    small[1].wait()
    diagonal = lax.broadcasted_iota(jnp.int32, (SUB, SUB), 0) == lax.broadcasted_iota(jnp.int32, (SUB, SUB), 1)
    for i in range(12):
        flips = (1 - 2 * sign_ref[:, i * SUB:(i + 1) * SUB]).astype(jnp.float32)
        scaled = jnp.where(diagonal, flips, 0.0).astype(jnp.bfloat16)
        weights[i // SIDE, i % SIDE] = jnp.dot(scaled, base, preferred_element_type=jnp.float32).astype(jnp.bfloat16)
    column = lax.broadcasted_iota(jnp.int32, (1, BLOCK), 1)
    ramp[...] = (((7919 * column) & (BLOCK - 1)).astype(jnp.float32) + 0.5) * (1.0 / BLOCK)

    def parts_of(views, b):
        parts = []
        for k in range(SIDE):
            values = jnp.concatenate([view[:, k * SUB:(k + 1) * SUB] for view in views], axis=0)
            parts.append(jnp.dot(values, weights[b, k], preferred_element_type=jnp.float32))
        return parts

    def peak_of(c, top):
        load(2 * c).wait()
        load(2 * c + 1).wait()
        for b in range(3):
            m = parts_of([held.at[2 * c + i, :, pl.ds(b * BLOCK, BLOCK)] for i in range(2)], b)
            even = jnp.abs(m[0] + m[1]) + jnp.abs(m[2] + m[3])
            odd = jnp.abs(m[0] - m[1]) + jnp.abs(m[2] - m[3])
            both = jnp.maximum(even, odd)
            both = jnp.maximum(both[:, :LANES], both[:, LANES:])
            top = jnp.maximum(top, jnp.max(both.reshape(36, 8, LANES), axis=0))
        return top

    top = lax.fori_loop(0, SIDE * 2, peak_of, jnp.zeros((8, LANES), jnp.float32))

    def spread(source, target):
        for i in range(18):
            rows_of[i:i + 1, :] = source[:, lanes(i)].astype(jnp.float32) * (1.0 / BLOCK)
        turned = jnp.transpose(rows_of[...], (1, 0))
        for i in range(18):
            spread_rows = jnp.broadcast_to(turned[:, i:i + 1], (LANES, LANES))
            start = i * LANES
            while start < (i + 1) * LANES:
                c, r = start // 144, start % 144
                n = min(144 - r, (i + 1) * LANES - start)
                target[c, r:r + n, :] = spread_rows[start - i * LANES:start - i * LANES + n]
                start += n

    def peak_copy(source, target, i, peer):
        return pltpu.make_async_remote_copy(
            peak_send.at[source], target, peak_ss.at[i], peak_rs.at[i], device_id=peer, device_id_type=MESH)

    def from_core_1():
        return peak_copy(0, peak_recv.at[0], 0, partner)

    def to_core_1():
        return peak_copy(4, peak_all, 10, partner)

    def stage_copies(s):
        return [peak_copy(1 + s, peak_recv.at[1 + 3 * s + i], 1 + 3 * s + i, peer) for i, peer in enumerate(stages[s])]

    def start_stage(s, value):
        peak_send[1 + s] = value
        for copy in stage_copies(s):
            copy.start()

    def end_stage(s):
        value = peak_send[1 + s]
        for i, copy in enumerate(stage_copies(s)):
            copy.wait_recv()
            value = jnp.maximum(value, peak_recv[1 + 3 * s + i])
        return value

    peak_send[0] = top

    @pl.when(core == 1)
    def _():
        from_core_1().start()

    @pl.when(core == 0)
    def _():
        from_core_1().wait_recv()
        start_stage(0, jnp.maximum(peak_send[0], peak_recv[0]))
        send_late()

    spread(dither_ref, own_dither)
    for i in range(4):
        near_copies[i].wait_recv()
        spread(near_raw.at[i], near_dither.at[i])

    @pl.when(core == 0)
    def _():
        start_stage(1, end_stage(0))
        start_stage(2, end_stage(1))
        value = end_stage(2)
        peak_send[4] = value
        to_core_1().start()
        peak_all[...] = value

    @pl.when(core == 1)
    def _():
        to_core_1().wait_recv()

    top = peak_all[...]
    top = jnp.max(jnp.max(top, axis=1, keepdims=True), axis=0, keepdims=True)
    peak = jnp.broadcast_to(top, (8, LANES))
    peak_ref[0] = LEVELS / peak
    peak_ref[1] = peak / (LEVELS * 16 * BLOCK)

    def codes(views, b, offsets):
        values = butterfly(parts_of(views, b))
        offsets = jnp.concatenate(offsets, axis=0)
        scale = peak_ref[0, 0:1, :]
        result = []
        for i in range(8):
            shift = offsets + ramp[:, lanes(i)]
            shift = shift - jnp.floor(shift)
            value = values[i // 2][:, (i % 2) * LANES:(i % 2 + 1) * LANES]
            result.append(jnp.floor(value * scale + shift))
        return result

    def own_codes(h, here, j, b, r0, n):
        targets = [target_of(h, here, j + jj) for jj in range(2)]
        rows = pl.ds(r0, n)
        return codes([held.at[c, rows, pl.ds(b * BLOCK, BLOCK)] for c in targets], b, [own_dither[c, rows, :] for c in targets])

    def near_codes(buffer, first, h, e, here, j, b, r0, n):
        targets = [target_of(h, here, j + jj) for jj in range(2)]
        views = [buffer.at[e, jj, pl.ds(first, n), :] for jj in range(2)]
        return codes(views, b, [near_dither[2 * h + e, c, pl.ds(r0, n), :] for c in targets])

    first_copies = {}

    def first(p):
        h, b, r0, n, q = PIECES[p]
        here = spots(h)[0]
        rows = pl.ds(q, n)
        for e in range(2):
            target = (here + 2 * e + 3) % SIDE
            for copy in raw_copies(p, e):
                copy.wait_recv()
            mine = own_codes(h, target, 2 * e, b, r0, n)
            other = near_codes(raw, q, h, e, target, 2 * e, b, r0, n)
            for i in range(8):
                total = (mine[i] + other[i]).astype(jnp.bfloat16)
                first_send[e, pl.ds(2 * e, 2), rows, lanes(i)] = total.reshape(2, n, LANES)
            if p not in LEAVES:
                mine = own_codes(h, target, 2 * (1 - e), b, r0, n)
                for i in range(8):
                    first_send[e, pl.ds(2 * (1 - e), 2), rows, lanes(i)] = mine[i].astype(jnp.bfloat16).reshape(2, n, LANES)
            sent = pl.ds(2 * e, 2) if p in LEAVES else slice(None)
            copy = pltpu.make_async_remote_copy(
                first_send.at[e, sent, rows, :], first_recv.at[e, sent, rows, :],
                first_ss.at[2 * p + e], first_rs.at[2 * p + e],
                device_id=neighbour(turns[h], 2 * e - 1), device_id_type=MESH)
            copy.start()
            first_copies[2 * p + e] = copy

    mid_copies, last_copies = {}, {}

    def combine(p):
        h, b, r0, n, q = PIECES[p]
        here, there = spots(h)
        rows = pl.ds(q, n)
        for e in range(2):
            first_copies[2 * p + e].wait_recv()

        def fill(half):
            pair = pl.ds(2 * half, 2)
            mine = own_codes(h, here, 2 * half, b, r0, n)
            if p in LEAVES:
                mine_too = near_codes(leaf, LEAVES[p], h, 1 - half, here, 2 * half, b, r0, n)
            for i in range(8):
                total = mine[i]
                if p in LEAVES:
                    total += mine_too[i] + first_recv[half, pair, rows, lanes(i)].astype(jnp.float32).reshape(2 * n, LANES)
                else:
                    for e in range(2):
                        total += first_recv[e, pair, rows, lanes(i)].astype(jnp.float32).reshape(2 * n, LANES)
                partial[pair, rows, lanes(i)] = total.astype(jnp.int32).astype(jnp.int16).reshape(2, n, LANES)

        def send():
            for e in range(2):
                copy = pltpu.make_async_remote_copy(
                    partial.at[(there + 2) % SIDE, rows, pl.ds(512 * e, 512)], second_raw.at[e, rows, :],
                    mid_ss.at[2 * p + e], mid_rs.at[2 * p + e],
                    device_id=neighbour(1 - turns[h], 2 * e - 1), device_id_type=MESH)
                copy.start()
                mid_copies[2 * p + e] = copy

        if p in LEAVES:
            for e in range(2):
                for copy in leaf_copies(p, e):
                    copy.wait_recv()
            fill(0)
            fill(1)
            send()
        else:
            opposite = (there + 2) % SIDE // 2
            fill(opposite)
            send()
            fill(1 - opposite)

    def forward(p):
        h, b, r0, n, q = PIECES[p]
        there = spots(h)[1]
        rows = pl.ds(q, n)
        for e in range(2):
            mid_copies[2 * p + e].wait_recv()
            j = (there + 2 * e + 3) % SIDE
            plain, summed = pl.ds(512 * (1 - e), 512), pl.ds(512 * e, 512)
            second_send[e, rows, plain] = partial[j, rows, plain]
            total = partial[j, rows, summed].astype(jnp.int32) + second_raw[e, rows, :].astype(jnp.int32)
            second_send[e, rows, summed] = total.astype(jnp.int16)
            copy = pltpu.make_async_remote_copy(
                second_send.at[e, rows, :], second_recv.at[e, rows, :],
                last_ss.at[2 * p + e], last_rs.at[2 * p + e],
                device_id=neighbour(1 - turns[h], 2 * e - 1), device_id_type=MESH)
            copy.start()
            last_copies[2 * p + e] = copy

    def decode(p):
        h, b, r0, n, q = PIECES[p]
        there = spots(h)[1]
        rows = pl.ds(q, n)
        for e in range(2):
            last_copies[2 * p + e].wait_recv()
        parts = []
        for k in range(SIDE):
            cols = pl.ds(k * SUB, SUB)
            total = partial[there, rows, cols].astype(jnp.int32)
            for e in range(2):
                total += second_recv[e, rows, cols].astype(jnp.int32)
            total = total.astype(jnp.float32)
            high = total.astype(jnp.bfloat16)
            low = (total - high.astype(jnp.float32)).astype(jnp.bfloat16)
            parts.append(jnp.dot(high, table[...], preferred_element_type=jnp.float32)
                         + jnp.dot(low, table[...], preferred_element_type=jnp.float32))
        values = butterfly(parts)
        factor = peak_ref[1, 0:1, :]
        for i in range(8):
            col = b * BLOCK + i * LANES
            flips = (1 - 2 * sign_ref[:, col:col + LANES]).astype(jnp.float32)
            value = values[i // 2][:, (i % 2) * LANES:(i % 2 + 1) * LANES]
            out_ref[r0:r0 + n, col:col + LANES] = (value * factor * flips).astype(jnp.bfloat16)

    tasks = (first, combine, forward, decode)
    for kind, step in ORDER:
        for p in (2 * step, 2 * step + 1):
            if p < len(PIECES):
                tasks[kind](p)
    for copies in (first_copies, mid_copies, last_copies):
        for copy in copies.values():
            copy.wait_send()
    for e in range(2):
        for copy in sum([raw_copies(p, e) for p in range(len(PIECES))], []) + sum([leaf_copies(p, e) for p in LEAVES], []):
            copy.wait_send()
    for copy in near_copies:
        copy.wait_send()

    @pl.when(core == 0)
    def _():
        for s in range(3):
            for copy in stage_copies(s):
                copy.wait_send()
        to_core_1().wait_send()

    @pl.when(core == 1)
    def _():
        from_core_1().wait_send()


def local(gradients, dither, sign_bits):
    row_count, col_count = gradients.shape[1:]
    grad = gradients.reshape(16, row_count // 16, col_count)
    vmem, dma = pltpu.VMEM, pltpu.SemaphoreType.DMA
    pieces = 2 * len(PIECES)
    return pl.pallas_call(
        kernel,
        out_shape=jax.ShapeDtypeStruct((row_count // 16, col_count), jnp.bfloat16),
        in_specs=[pl.BlockSpec(memory_space=pl.ANY)] * 2,
        out_specs=pl.BlockSpec(memory_space=pltpu.VMEM),
        scratch_shapes=[
            vmem((1, row_count), jnp.int32),
            vmem((1, col_count), jnp.int32),
            vmem((16, 144, col_count), jnp.bfloat16),
            vmem((3, SIDE, SUB, SUB), jnp.bfloat16),
            vmem((SUB, SUB), jnp.bfloat16),
            vmem((16, 144, LANES), jnp.float32),
            vmem((4, 1, row_count), jnp.int32),
            vmem((4, 16, 144, LANES), jnp.float32),
            vmem((24, LANES), jnp.float32),
            vmem((1, BLOCK), jnp.float32),
            vmem((5, 8, LANES), jnp.float32),
            vmem((10, 8, LANES), jnp.float32),
            vmem((8, LANES), jnp.float32),
            vmem((2, 8, LANES), jnp.float32),
            vmem((2, 2, ROWS, BLOCK), jnp.bfloat16),
            vmem((2, 2, LEAF_ROWS, BLOCK), jnp.bfloat16),
            vmem((2, SIDE, ROWS, BLOCK), jnp.bfloat16),
            vmem((2, SIDE, ROWS, BLOCK), jnp.bfloat16),
            vmem((SIDE, ROWS, BLOCK), jnp.int16),
            vmem((2, ROWS, 512), jnp.int16),
            vmem((2, ROWS, BLOCK), jnp.int16),
            vmem((2, ROWS, BLOCK), jnp.int16),
            dma((2,)), dma((16,)), dma((4,)), dma((4,)), dma((11,)), dma((11,)), dma((2 * pieces,)), dma((2 * pieces,)),
            dma((4 * len(LEAVES),)), dma((4 * len(LEAVES),)), dma((pieces,)), dma((pieces,)), dma((pieces,)), dma((pieces,)), dma((pieces,)), dma((pieces,)),
        ],
        compiler_params=pltpu.CompilerParams(collective_id=0, has_side_effects=True, vmem_limit_bytes=50 * 2**20),
    )(grad, jnp.concatenate([dither, sign_bits.reshape(1, col_count)], axis=1))


def solution(mesh):
    return jax.shard_map(
        local,
        mesh=mesh,
        in_specs=(P("dp", None, "tensor"), P("dp", None), P("tensor")),
        out_specs=P("dp", "tensor"),
        check_vma=False,
    )
```

time: 89.4 us -> 84.6 us (0.946)
  Pallas kernels: 86.7 us -> 82.8 us
  local copies, waits for them, and re-layouts: 2.32 us -> 0.91 us
    pallas_call x1, Pallas kernels: 86.7 us -> 82.8 us  [local(): pl.pallas_call(kernel, out_shape=jax.ShapeDtypeStruct((row_count // 16, c...]
    unnamed x5 -> x1, local copies, waits for them, and re-layouts: 2.32 us -> 0.91 us
where the time goes in v3:
time: 84.6 us; the launch traced here: 84.4 us
  Pallas kernels  82.8 us (98%)
  local copies, waits for them, and re-layouts  0.91 us (1%)
    pallas_call x1, Pallas kernels, local(): pl.pallas_call(kernel, out_shape=jax.ShapeDtypeStruct((row_count // 16, c...  82.8 us

profile of v3, /device:TPU:0, one launch (start us, length us, event | category | flops | bytes accessed | tf_op | source)
XLA Modules:
  0.0 84.4 jit_solution(11504311416057371471)
XLA Ops:
  0.0 0.7 pad_add_fusion.small_in
  0.7 82.8 %shard_map.37 = bf16[144,3072]{1,0:T(8,128)(2,1)S(1)} custom-call(bf16[16,144,3072]{2,1,0:T(8,128)(2,1)} %bitcast.2, s32[1,5376]{1,0:T(1,128)S(1)} %pad_add_fusion.small_in), custom_call_target="tpu_custom_call" | custom-call | tf_op jit(solution)/shard_map/pallas_call | solution.py:420
  83.5 0.9 %copy.5 = bf16[144,3072]{1,0:T(8,128)(2,1)} copy(bf16[144,3072]{1,0:T(8,128)(2,1)S(1)} %shard_map.37) | data formatting | bytes 1769472

commit v4 on v3

--- a/solution.py
+++ b/solution.py
@@ -35,7 +35,7 @@
     return [a + c, b + d, a - c, b - d]
 
 
-def kernel(grad, small_in, out_ref, dither_ref, sign_ref, held, weights, table, own_dither, near_raw, near_dither, rows_of, ramp, peak_send,
+def kernel(grad, small_in, out_ref, dither_ref, sign_ref, held, weights, table, own_dither, near_raw, near_dither, own_rows, ramp, peak_send,
            peak_recv, peak_all, peak_ref, raw, leaf, first_send, first_recv, partial, second_raw, second_send, second_recv,
            small_sem, load_sem, near_ss, near_rs, peak_ss, peak_rs, raw_ss, raw_rs, leaf_ss, leaf_rs, first_ss, first_rs, mid_ss, mid_rs, last_ss, last_rs):
     dp, tensor = lax.axis_index("dp"), lax.axis_index("tensor")
@@ -127,10 +127,13 @@
         send_raw(p)
     lax.fori_loop(0, SIDE * SIDE, start_load, 0)
     small[0].wait()
+    own_rows[...] = jnp.zeros_like(own_rows)
+    for i in range(18):
+        own_rows[i:i + 1, :] = dither_ref[:, lanes(i)]
     near_copies = []
     for i in range(4):
         copy = pltpu.make_async_remote_copy(
-            dither_ref, near_raw.at[i], near_ss.at[i], near_rs.at[i],
+            own_rows, near_raw.at[i], near_ss.at[i], near_rs.at[i],
             device_id=neighbour(turns[i // 2], 2 * (i % 2) - 1), device_id_type=MESH)
         copy.start()
         near_copies.append(copy)
@@ -176,9 +179,7 @@
     top = lax.fori_loop(0, SIDE * 2, peak_of, jnp.zeros((8, LANES), jnp.float32))
 
     def spread(source, target):
-        for i in range(18):
-            rows_of[i:i + 1, :] = source[:, lanes(i)].astype(jnp.float32) * (1.0 / BLOCK)
-        turned = jnp.transpose(rows_of[...], (1, 0))
+        turned = jnp.transpose(source[...].astype(jnp.float32) * (1.0 / BLOCK), (1, 0))
         for i in range(18):
             spread_rows = jnp.broadcast_to(turned[:, i:i + 1], (LANES, LANES))
             start = i * LANES
@@ -225,7 +226,7 @@
         start_stage(0, jnp.maximum(peak_send[0], peak_recv[0]))
         send_late()
 
-    spread(dither_ref, own_dither)
+    spread(own_rows, own_dither)
     for i in range(4):
         near_copies[i].wait_recv()
         spread(near_raw.at[i], near_dither.at[i])
@@ -429,9 +430,9 @@
             vmem((3, SIDE, SUB, SUB), jnp.bfloat16),
             vmem((SUB, SUB), jnp.bfloat16),
             vmem((16, 144, LANES), jnp.float32),
-            vmem((4, 1, row_count), jnp.int32),
+            vmem((4, 24, LANES), jnp.int32),
             vmem((4, 16, 144, LANES), jnp.float32),
-            vmem((24, LANES), jnp.float32),
+            vmem((24, LANES), jnp.int32),
             vmem((1, BLOCK), jnp.float32),
             vmem((5, 8, LANES), jnp.float32),
             vmem((10, 8, LANES), jnp.float32),

time: 84.6 us -> 84.7 us (level)
  no operation moved by 1% of the time
where the time goes in v4:
time: 84.7 us; the launch traced here: 84.5 us
  Pallas kernels  82.9 us (98%)
  local copies, waits for them, and re-layouts  0.91 us (1%)
    pallas_call x1, Pallas kernels, local(): pl.pallas_call(kernel, out_shape=jax.ShapeDtypeStruct((row_count // 16, c...  82.9 us

profile of v4, /device:TPU:0, one launch (start us, length us, event | category | flops | bytes accessed | tf_op | source)
XLA Modules:
  0.0 84.5 jit_solution(16937542388517807719)
XLA Ops:
  0.0 0.7 pad_add_fusion.small_in
  0.7 82.9 %shard_map.37 = bf16[144,3072]{1,0:T(8,128)(2,1)S(1)} custom-call(bf16[16,144,3072]{2,1,0:T(8,128)(2,1)} %bitcast.2, s32[1,5376]{1,0:T(1,128)S(1)} %pad_add_fusion.small_in), custom_call_target="tpu_custom_call" | custom-call | tf_op jit(solution)/shard_map/pallas_call | solution.py:421
  83.6 0.9 %copy.5 = bf16[144,3072]{1,0:T(8,128)(2,1)} copy(bf16[144,3072]{1,0:T(8,128)(2,1)S(1)} %shard_map.37) | data formatting | bytes 1769472
